TPU v7x, 256 devices: a whole 4x4x8 slice. The times are simulated.
256 devices in a mesh: prow: 32 (over y, x, core), pcol: 8 (over z).
Axes of the slice: x: 4, y: 4, z: 8, core: 2. Of those that a mesh axis runs over, the one named last changes fastest.
Arguments:
- eigvecs: float32 [65536, 4096], P('prow', 'pcol'), may hold values from -6 to 6
- reflectors: float32 [65536, 512], P('prow', 'pcol'), may hold values from -0.25 to 0.25
- factors: float32 [512, 256], P('pcol'), may hold values from -1 to 2, as said below
Outputs:
- result_vectors: float32 [65536, 4096], P('prow', 'pcol')
Inputs may be any that keep to these rules, and one draw needn't show every extreme that they name: `factors`: within each block of 256 rows the factor is upper triangular, its diagonal between 1 and 2.
All inputs are finite; a program needn't handle non-finite values.
Results may differ from a plain program's by a relative error of at most 0.00017.
Values sent between devices are 32-bit elements; how exact they have to be, the bound alone decides.
A program may use at most 64 MiB of HBM per device.

v0:
```python
import jax
import jax.numpy as jnp
from jax import lax
from jax.sharding import PartitionSpec as P


def contract_rows(left, right):
    return lax.dot_general(
        left,
        right,
        (((0,), (0,)), ((), ())),
        precision=lax.Precision.HIGHEST,
        preferred_element_type=jnp.float32,
    )


def product(left, right):
    return jnp.dot(left, right, precision=lax.Precision.HIGHEST, preferred_element_type=jnp.float32)


def shards(eigvecs, reflectors, factors):
    panel, triangle = (
        lax.all_gather(reflectors, "pcol", axis=1, tiled=True),
        lax.all_gather(factors, "pcol", axis=0, tiled=True),
    )
    block_width = triangle.shape[1]
    block_count = triangle.shape[0] // block_width
    vectors = eigvecs
    for index in range(block_count - 1, -1, -1):
        block_panel = panel[:, index * block_width : (index + 1) * block_width]
        block_factor = triangle[index * block_width : (index + 1) * block_width]
        partial_value = contract_rows(block_panel, vectors)
        summed = lax.psum(partial_value, "prow")
        coeffs = product(block_factor, summed)
        vectors = vectors - product(block_panel, coeffs)
    return vectors


def solution(mesh):
    return jax.shard_map(
        shards,
        mesh=mesh,
        in_specs=(P("prow", "pcol"), P("prow", "pcol"), P("pcol", None)),
        out_specs=P("prow", "pcol"),
        check_vma=False,
    )
```

profile of v0, /device:TPU:1, one launch (start us, length us, event | category | flops | bytes accessed | tf_op | source)
XLA Modules:
  0.0 336.3 jit_solution(86224858127432723)
XLA Ops:
  6.5 0.0 all-gather.2.cloned.1.call-start
  6.5 0.7 all-gather.2.cloned.1.call-update
  7.3 0.0 all-reduce.3.cloned.1.call-start
  7.3 60.5 %all-gather.2.cloned.1.call-done = f32[2048,512]{0,1:T(8,128)} async-done(((f32[2048,64]{0,1:T(8,128)}), f32[2048,512]{0,1:T(8,128)}) %all-gather.2.cloned.1.call-update) | async-done | bytes 4194320 | tf_op jit(solution)/shard_map/all_gather | solution.py:23
  67.8 7.3 %fusion.4 = f32[256,512]{1,0:T(8,128)} fusion(f32[2048,512]{1,0:T(8,128)} %param.3, f32[2048,512]{0,1:T(8,128)} %all-gather.2.cloned.1.call-done), kind=kOutput, calls=%fused_computation.6 | convolution fusion | flops 3221225472 | bytes 6815744 | tf_op jit(solution)/shard_map/dot_general | solution.py:8
  75.1 0.0 all-reduce.3.cloned.1.call-update
  75.1 0.0 copy-start.2
  75.1 0.0 all-reduce.5.cloned.1.call-start
  75.2 5.3 %copy.4 = f32[2048,512]{0,1:T(8,128)} copy(f32[2048,512]{1,0:T(8,128)} %param.3) | data formatting | bytes 8388608 | tf_op args[0]
  80.5 0.0 copy-done.2
  80.5 19.8 %all_gather.7 = f32[512,256]{1,0:T(8,128)S(1)} all-gather(f32[64,256]{1,0:T(8,128)S(1)} %copy-done.2), channel_id=1, replica_groups=mesh['prow'=32,'pcol'=8] {'pcol'}, dimensions={0}, use_global_device_ids=true | all-gather | bytes 589824 | tf_op jit(solution)/shard_map/all_gather | solution.py:24
  100.4 87.1 %all-reduce.3.cloned.1.call-done = f32[256,512]{1,0:T(8,128)} async-done(((f32[256,512]{1,0:T(8,128)}), f32[256,512]{1,0:T(8,128)}) %all-reduce.3.cloned.1.call-update) | async-done | bytes 524304 | tf_op jit(solution)/shard_map/psum | solution.py:33
  187.4 2.0 fusion.11
  189.5 0.0 copy-start.1
  189.5 6.3 %bitcast_subtract_fusion.1 = f32[2048,512]{0,1:T(8,128)S(1)} fusion(f32[2048,512]{0,1:T(8,128)} %copy.4, f32[512,256]{1,0:T(8,128)S(1)} %fusion.11, f32[2048,512]{0,1:T(8,128)} %all-gather.2.cloned.1.call-done), kind=kOutput, calls=%fused_computation.1 | convolution fusion | flops 3222274048 | bytes 11010048 | tf_op jit(solution)/shard_map/dot_general | solution.py:18
  195.8 0.0 copy-start
  195.8 2.0 copy-done
  197.8 0.0 copy-done.1
  197.8 4.3 %fusion.6 = f32[256,512]{0,1:T(8,128)} fusion(f32[2048,512]{0,1:T(8,128)S(1)} %bitcast_subtract_fusion.1, f32[2048,512]{0,1:T(8,128)S(1)} %copy-done.1), kind=kOutput, calls=%fused_computation.8 | convolution fusion | flops 3221225472 | bytes 6815744 | tf_op jit(solution)/shard_map/dot_general | solution.py:8
  202.1 0.0 all-reduce.5.cloned.1.call-update
  202.1 113.3 %all-reduce.5.cloned.1.call-done = f32[256,512]{0,1:T(8,128)} async-done(((f32[256,512]{0,1:T(8,128)}), f32[256,512]{0,1:T(8,128)}) %all-reduce.5.cloned.1.call-update) | async-done | bytes 524304 | tf_op jit(solution)/shard_map/psum | solution.py:33
  315.4 1.7 fusion.9
  317.1 7.4 %bitcast_subtract_fusion = f32[2048,512]{0,1:T(8,128)} fusion(f32[2048,512]{0,1:T(8,128)} %copy-done, f32[512,256]{1,0:T(8,128)S(1)} %fusion.9, f32[2048,512]{0,1:T(8,128)} %all-gather.2.cloned.1.call-done), kind=kOutput, calls=%fused_computation | convolution fusion | flops 3222274048 | bytes 11010048 | tf_op jit(solution)/shard_map/dot_general | solution.py:18
  324.5 5.3 %copy.5 = f32[2048,512]{1,0:T(8,128)} copy(f32[2048,512]{0,1:T(8,128)} %bitcast_subtract_fusion) | data formatting | bytes 8388608 | tf_op jit(solution)/shard_map/sub | solution.py:35
Async XLA Ops:
  6.5 61.3 %all-gather.2.cloned.1.call-start = ((), (), s32[]{:S(2)}) async-start(), calls=%async_computation | async-start | bytes 4718592 | tf_op jit(solution)/shard_map/all_gather | solution.py:23
  7.3 180.2 %all-reduce.3.cloned.1.call-start = ((), (), s32[]{:S(2)}) async-start(), calls=%async_computation.1 | async-start | bytes 1048576 | tf_op jit(solution)/shard_map/psum | solution.py:33
  75.1 5.4 %copy-start.2 = (f32[64,256]{1,0:T(8,128)S(1)}, f32[64,256]{1,0:T(8,128)}, u32[]{:S(2)}) copy-start(f32[64,256]{1,0:T(8,128)} %param.5) | copy-start | bytes 196612
  75.1 240.3 %all-reduce.5.cloned.1.call-start = ((), (), s32[]{:S(2)}) async-start(), calls=%async_computation.2 | async-start | bytes 1048576 | tf_op jit(solution)/shard_map/psum | solution.py:33
  189.5 8.4 %copy-start.1 = (f32[2048,512]{0,1:T(8,128)S(1)}, f32[2048,512]{0,1:T(8,128)}, u32[]{:S(2)}) copy-start(f32[2048,512]{0,1:T(8,128)} %all-gather.2.cloned.1.call-done) | copy-start | bytes 12582916
  195.8 2.0 copy-start
Sparse Core Ops, SparseCore 0:
  9.1 58.6 all-gather.1
  75.3 112.1 all-reduce.2
  202.3 113.1 all-reduce.4
where the time goes:
time: 337 us; the launch traced here: 336 us
  waiting for transfers between devices  262 us (78%)
  matrix products  29 us (9%)
  blocking collectives  19.8 us (6%)
  between operations  13.2 us (4%)
  local copies, waits for them, and re-layouts  12.7 us (4%)
    psum x2, waiting for transfers between devices, shards(): summed = lax.psum(partial_value, 'prow')  200 us
    all_gather x1, waiting for transfers between devices, shards(): lax.all_gather(reflectors, 'pcol', axis=1, tiled=True)  60.5 us
    all_gather x1, blocking collectives, shards(): lax.all_gather(factors, 'pcol', axis=0, tiled=True)  19.8 us
    dot_general x4, matrix products, product(): jnp.dot(left, right, precision=lax.Precision.HIGHEST, preferred_element_t...  17.4 us
    dot_general x2, matrix products, contract_rows(): lax.dot_general(left, right, (((0,), (0,)), ((), ())), precision=lax.Prec...  11.6 us
    unnamed x7, local copies, waits for them, and re-layouts  7.37 us
  transfers between devices with their start and end apart: 3, of which 3 were waited for; matrix products, arithmetic and copies ran while one was open for 2% of the time, Pallas kernels for 0%

commit v1 on v0

v1 whole, which is shorter than its diff:
```python
import functools

import jax
import jax.numpy as jnp
from jax import lax
from jax.experimental import pallas as pl
from jax.experimental.pallas import tpu as pltpu
from jax.sharding import PartitionSpec as P

MESH = pl.DeviceIdType.MESH
F32, BF16 = jnp.float32, jnp.bfloat16
PLANES = 8
ROWS = 32
CHIPS = 16
SLAB = 64
PIECES = 2
NN = (((1,), (0,)), ((), ()))
NT = (((1,), (1,)), ((), ()))
TN = (((0,), (0,)), ((), ()))


def split(value):
    high = value.astype(BF16)
    return high, (value - high.astype(F32)).astype(BF16)


def product(left, right, dims):
    dot = functools.partial(lax.dot_general, dimension_numbers=dims, preferred_element_type=F32)
    return dot(left[0], right[0]) + (dot(left[1], right[0]) + dot(left[0], right[1]))


def kernel(
    z_hbm, v_hbm, t_hbm, out,
    panel, v_hi, v_lo, vt_hi, vt_lo, z_full, z_hi, z_lo, z_sum, gram,
    t_in, t_mine, t_planes, t_all, t_full, coeff, c_hi, c_lo,
    give_a, give_b, give_c, give_d, take_a, take_b, take_c, take_d, all_a, all_b, all_c, all_d,
    local, ring_out, ring_in, t_out, t_got, part_out, part_in,
):
    z, p = lax.axis_index("pcol"), lax.axis_index("prow")
    chip, core = p // 2, lax.rem(p, 2)
    right, left = lax.rem(z + 1, PLANES), lax.rem(z + PLANES - 1, PLANES)

    def plane(offset):
        return lax.rem(z + offset, PLANES)

    def mate(step):
        o = 20 + step
        o = o - 31 * (o // 32)
        y = lax.rem(p // 8 + o // 8, 4)
        x = lax.rem(chip + lax.rem(o // 2, 4), 4)
        return (y * 4 + x) * 2 + lax.rem(core + lax.rem(o, 2), 2)

    def fellow(step):
        o = 1 + step
        return (lax.rem(p // 8 + o // 4, 4) * 4 + lax.rem(chip + lax.rem(o, 4), 4)) * 2 + core

    barrier = pltpu.get_barrier_semaphore()
    for offset in range(1, PLANES):
        pl.semaphore_signal(barrier, inc=1, device_id={"pcol": plane(offset)}, device_id_type=MESH)

    def greet(step, carry):
        pl.semaphore_signal(barrier, inc=1, device_id={"prow": mate(step)}, device_id_type=MESH)
        return carry

    lax.fori_loop(0, ROWS - 1, greet, 0)
    own_copy = pltpu.make_async_copy(v_hbm, panel.at[z], local.at[0])
    t_copy = pltpu.make_async_copy(t_hbm, t_in, local.at[1])
    z_copy = pltpu.make_async_copy(z_hbm, z_full, local.at[2])
    own_copy.start()
    t_copy.start()
    z_copy.start()
    pl.semaphore_wait(barrier, PLANES - 1 + ROWS - 1)

    height = SLAB // PIECES

    def ring(way, step, piece):
        slab = plane(PLANES - step) if way == 0 else plane(step)
        ref = panel.at[slab, pl.ds(piece * height, height)]
        return pltpu.make_async_remote_copy(
            ref, ref, ring_out.at[way, step, piece], ring_in.at[way, step, piece],
            device_id={"pcol": right if way == 0 else left}, device_id_type=MESH,
        )

    def pieces(way, step):
        half = PIECES // 2
        if step < 3:
            return list(range(PIECES))
        return list(range(half)) if way == 0 else list(range(half, PIECES))

    def arrive(step):
        for piece in range(PIECES):
            for way in range(2):
                if piece in pieces(way, step):
                    ring(way, step, piece).wait_recv()
                if step < 3 and piece in pieces(way, step + 1):
                    ring(way, step + 1, piece).start()

    own_copy.wait()
    for piece in range(PIECES):
        for way in range(2):
            ring(way, 0, piece).start()

    t_copy.wait()
    for tile in range(CHIPS):
        t_mine[tile] = t_in[(tile // 2) * 8 : (tile // 2) * 8 + 8, (tile % 2) * 128 : (tile % 2) * 128 + 128]
    for offset in range(1, PLANES):
        pltpu.make_async_remote_copy(
            t_mine.at[chip], t_planes.at[z], t_out.at[0], t_got.at[0],
            device_id={"pcol": plane(offset)}, device_id_type=MESH,
        ).start()
    t_planes[z] = t_mine[chip]

    def t_wait(stage):
        ref = t_planes.at[pl.ds(0, PLANES - 1)] if stage == 0 else t_all.at[pl.ds(0, CHIPS - 1)]
        return pltpu.make_async_remote_copy(
            ref, ref, t_out.at[stage], t_got.at[stage], device_id={"pcol": right}, device_id_type=MESH
        )

    def t_spread():
        t_wait(0).wait_recv()

        def send(step, carry):
            pltpu.make_async_remote_copy(
                t_planes, t_all.at[chip], t_out.at[1], t_got.at[1],
                device_id={"prow": fellow(step)}, device_id_type=MESH,
            ).start()
            return carry

        lax.fori_loop(0, CHIPS - 1, send, 0)
        t_all[chip] = t_planes[...]

    def t_collect():
        t_wait(1).wait_recv()
        for tile in range(CHIPS):
            for slab in range(PLANES):
                t_full[
                    slab * SLAB + (tile // 2) * 8 : slab * SLAB + (tile // 2) * 8 + 8,
                    (tile % 2) * 128 : (tile % 2) * 128 + 128,
                ] = t_all[tile, slab]

    gives, takes, alls = (give_a, give_b, give_c, give_d), (take_a, take_b, take_c, take_d), (all_a, all_b, all_c, all_d)

    def part_wait(part, stage):
        ref = (takes, alls)[stage][part].at[pl.ds(0, ROWS - 1)]
        return pltpu.make_async_remote_copy(
            ref, ref, part_out.at[part, stage], part_in.at[part, stage],
            device_id={"pcol": right}, device_id_type=MESH,
        )

    def part_give(part):
        def send(step, carry):
            other = mate(step)
            pltpu.make_async_remote_copy(
                gives[part].at[other], takes[part].at[p], part_out.at[part, 0], part_in.at[part, 0],
                device_id={"prow": other}, device_id_type=MESH,
            ).start()
            return carry

        lax.fori_loop(0, ROWS - 1, send, 0)
        takes[part][p] = gives[part][p]

    def part_sum(part):
        part_wait(part, 0).wait_recv()
        alls[part][p] = jnp.sum(takes[part][...], axis=0)

        def send(step, carry):
            pltpu.make_async_remote_copy(
                alls[part].at[p], alls[part].at[p], part_out.at[part, 1], part_in.at[part, 1],
                device_id={"prow": mate(step)}, device_id_type=MESH,
            ).start()
            return carry

        lax.fori_loop(0, ROWS - 1, send, 0)

    def halves(slab):
        v_hi[slab], v_lo[slab] = split(panel[slab])

    def others(slab):
        at = pl.ds(4 - 4 * (slab // 4), 4)
        return v_hi[at].reshape(4 * SLAB, -1), v_lo[at].reshape(4 * SLAB, -1)

    def gram_of(slab):
        return product((v_hi[slab], v_lo[slab]), others(slab), NT)

    def sums_of(slabs):
        rows = len(slabs) * SLAB
        high = [v_hi[slab] for slab in slabs]
        low = [v_lo[slab] for slab in slabs]
        by_high = lax.dot_general(jnp.concatenate(high + low, axis=0), z_hi[...], NN, preferred_element_type=F32)
        by_low = lax.dot_general(jnp.concatenate(high, axis=0), z_lo[...], NN, preferred_element_type=F32)
        return by_high[:rows] + (by_high[rows:] + by_low)

    def lay_sums(part, values):
        for index in range(values.shape[0] // SLAB):
            for tile in range(ROWS):
                row, lane = index * SLAB + (tile // 4) * 8, (tile % 4) * 128
                gives[part][tile, index * 8 : index * 8 + 8] = values[row : row + 8, lane : lane + 128]

    def lay_gram(part, first, values, index):
        for tile in range(16):
            row, lane = (tile // 2) * 8, (tile % 2) * 128
            gives[part][index * 16 + tile, first : first + 8] = values[row : row + 8, lane : lane + 128]

    def collect(part, slabs):
        part_wait(part, 1).wait_recv()
        count = len(slabs)
        for index, slab in enumerate(slabs):
            for tile in range(ROWS):
                row, lane = (tile // 4) * 8, (tile % 4) * 128
                z_sum[slab, row : row + 8, lane : lane + 128] = alls[part][tile, index * 8 : index * 8 + 8]
        if part < 3:
            for index, slab in enumerate(slabs[-2:]):
                for tile in range(16):
                    row, lane = (tile // 2) * 8, (tile % 2) * 128
                    gram[slab, row : row + 8, lane : lane + 128] = alls[part][
                        index * 16 + tile, count * 8 : count * 8 + 8
                    ]
        else:
            for tile in range(32):
                row, lane = (tile // 4) * 8 + (tile % 2) * 4, (tile // 2 % 2) * 128
                gram[slabs[0], row : row + 4, lane : lane + 128] = alls[part][tile, 8:12]

    def turn(at, slabs):
        for target, source in ((vt_hi, v_hi), (vt_lo, v_lo)):
            target[:, at * 128 : at * 128 + 128] = jnp.concatenate([source[slab] for slab in slabs], axis=0).T

    late = plane(4)
    v_hi[...] = jnp.zeros_like(v_hi)
    v_lo[...] = jnp.zeros_like(v_lo)
    gram[z] = jnp.zeros_like(gram[z])
    halves(z)
    z_copy.wait()
    z_hi[...], z_lo[...] = split(z_full[...])

    for step in range(3):
        pair = [plane(PLANES - 1 - step), plane(1 + step)]
        slabs = [z, *pair] if step == 0 else pair
        arrive(step)
        halves(pair[0])
        first = gram_of(pair[0])
        halves(pair[1])
        second = gram_of(pair[1])
        lay_sums(step, sums_of(slabs))
        lay_gram(step, len(slabs) * 8, first, 0)
        lay_gram(step, len(slabs) * 8, second, 1)
        part_give(step)
        if step == 0:
            t_spread()
        if step == 1:
            t_collect()
        if step < 2:
            turn(step + 1, pair)
            part_sum(step)

    arrive(3)
    halves(late)
    grams = gram_of(late)
    lay_sums(3, sums_of([late]))
    for tile in range(32):
        row, lane = (tile // 4) * 8 + (tile % 2) * 4, (tile // 2 % 2) * 128
        give_d[tile, 8:12] = grams[row : row + 4, lane : lane + 128]
    part_give(3)
    part_sum(2)
    turn(0, [z, late])
    turn(3, [plane(5), plane(3)])
    collect(0, [z, plane(7), plane(1)])
    collect(1, [plane(6), plane(2)])
    part_sum(3)
    collect(2, [plane(5), plane(3)])
    t_hi, t_lo = split(t_full[...])
    collect(3, [late])

    sums = z_sum[...].reshape(512, -1)
    grams = split(gram[...].reshape(512, 256))
    second = product((t_hi[256:], t_lo[256:]), split(sums[256:]), NN)
    halved = split(second)
    crossed = product((grams[0][:256], grams[1][:256]), halved, NN) + product(
        (grams[0][256:], grams[1][256:]), halved, TN
    )
    first = product((t_hi[:256], t_lo[:256]), split(sums[:256] - crossed), NN)
    coeff[pl.ds(0, 4)] = first.reshape(4, SLAB, -1)
    coeff[pl.ds(4, 4)] = second.reshape(4, SLAB, -1)
    for index, offset in enumerate((0, 4, 7, 1, 6, 2, 5, 3)):
        high, low = split(coeff[plane(offset)])
        c_hi[index * SLAB : index * SLAB + SLAB] = high
        c_lo[index * SLAB : index * SLAB + SLAB] = low

    def finish(block, carry):
        at = pl.ds(pl.multiple_of(block * 256, 256), 256)
        update = product((vt_hi[at], vt_lo[at]), (c_hi[...], c_lo[...]), NN)
        out[at] = z_full[at] - update
        return carry

    lax.fori_loop(0, z_full.shape[0] // 256, finish, 0)

    for step in range(4):
        for way in range(2):
            for piece in pieces(way, step):
                ring(way, step, piece).wait_send()
    t_wait(0).wait_send()
    t_wait(1).wait_send()
    for part in range(4):
        part_wait(part, 0).wait_send()
        part_wait(part, 1).wait_send()


def shards(eigvecs, reflectors, factors):
    rows, columns = eigvecs.shape
    heights = (32, 24, 24, 12)
    scratch = [
        pltpu.VMEM((PLANES, SLAB, rows), F32),
        pltpu.VMEM((PLANES, SLAB, rows), BF16),
        pltpu.VMEM((PLANES, SLAB, rows), BF16),
        pltpu.VMEM((rows, PLANES * SLAB), BF16),
        pltpu.VMEM((rows, PLANES * SLAB), BF16),
        pltpu.VMEM((rows, columns), F32),
        pltpu.VMEM((rows, columns), BF16),
        pltpu.VMEM((rows, columns), BF16),
        pltpu.VMEM((PLANES, SLAB, columns), F32),
        pltpu.VMEM((PLANES, SLAB, 256), F32),
        pltpu.VMEM((SLAB, 256), F32),
        pltpu.VMEM((CHIPS, 8, 128), F32),
        pltpu.VMEM((PLANES, 8, 128), F32),
        pltpu.VMEM((CHIPS, PLANES, 8, 128), F32),
        pltpu.VMEM((PLANES * SLAB, 256), F32),
        pltpu.VMEM((PLANES, SLAB, columns), F32),
        pltpu.VMEM((PLANES * SLAB, columns), BF16),
        pltpu.VMEM((PLANES * SLAB, columns), BF16),
        *[pltpu.VMEM((ROWS, height, 128), F32) for _ in range(3) for height in heights],
        pltpu.SemaphoreType.DMA((3,)),
        pltpu.SemaphoreType.DMA((2, 4, PIECES)),
        pltpu.SemaphoreType.DMA((2, 4, PIECES)),
        pltpu.SemaphoreType.DMA((2,)),
        pltpu.SemaphoreType.DMA((2,)),
        pltpu.SemaphoreType.DMA((4, 2)),
        pltpu.SemaphoreType.DMA((4, 2)),
    ]
    return pl.pallas_call(
        kernel,
        out_shape=jax.ShapeDtypeStruct(eigvecs.shape, F32),
        in_specs=[pl.BlockSpec(memory_space=pl.ANY)] * 3,
        out_specs=pl.BlockSpec(memory_space=pltpu.VMEM),
        scratch_shapes=scratch,
        compiler_params=pltpu.CompilerParams(
            collective_id=0, has_side_effects=True, vmem_limit_bytes=48 * 1024 * 1024
        ),
    )(eigvecs, reflectors.T, factors)


def solution(mesh):
    return jax.shard_map(
        shards,
        mesh=mesh,
        in_specs=(P("prow", "pcol"), P("prow", "pcol"), P("pcol", None)),
        out_specs=P("prow", "pcol"),
        check_vma=False,
    )
```

time: 337 us -> 87 us (0.26)
  waiting for transfers between devices: 262 us -> 0 us
  Pallas kernels: 0 us -> 82.9 us
  matrix products: 29 us -> 0 us
  blocking collectives: 19.8 us -> 0 us
  between operations: 13.2 us -> 0.01 us
  local copies, waits for them, and re-layouts: 12.7 us -> 3.9 us
    psum x2 -> x0, waiting for transfers between devices: 200 us -> none  [shards(): summed = lax.psum(partial_value, 'prow')]
    pallas_call x0 -> x1, Pallas kernels: none -> 82.9 us  [shards(): pl.pallas_call(kernel, out_shape=jax.ShapeDtypeStruct(eigvecs.shape, F32)...]
    all_gather x1 -> x0, waiting for transfers between devices: 60.5 us -> none  [shards(): lax.all_gather(reflectors, 'pcol', axis=1, tiled=True)]
    dot_general x6 -> x0, matrix products: 29 us -> none  [the longest x4 17.4 us: product(): jnp.dot(left, right, precision=lax.Precision.HIGHEST, preferred_element_t...]
    all_gather x1 -> x0, blocking collectives: 19.8 us -> none  [shards(): lax.all_gather(factors, 'pcol', axis=0, tiled=True)]
    sub x1 -> x0, local copies, waits for them, and re-layouts: 5.34 us -> none  [shards(): vectors = vectors - product(block_panel, coeffs)]
    unnamed x7 -> x5, local copies, waits for them, and re-layouts: 7.37 us -> 3.9 us
  transfers between devices with their start and end apart: 3 -> 0, of which waited for: 3 -> 0; matrix products, arithmetic and copies ran while one was open for 2% -> 0% of each run, Pallas kernels for 0% -> 0%
where the time goes in v1:
time: 87 us; the launch traced here: 86.8 us
  Pallas kernels  82.9 us (95%)
  local copies, waits for them, and re-layouts  3.9 us (4%)
    pallas_call x1, Pallas kernels, shards(): pl.pallas_call(kernel, out_shape=jax.ShapeDtypeStruct(eigvecs.shape, F32)...  82.9 us
    unnamed x5, local copies, waits for them, and re-layouts  3.9 us

profile of v1, /device:TPU:1, one launch (start us, length us, event | category | flops | bytes accessed | tf_op | source)
XLA Modules:
  0.0 86.8 jit_solution(5624465539838441136)
XLA Ops:
  0.0 0.0 copy-start
  0.0 1.0 %copy-done = f32[2048,64]{0,1:T(8,128)S(1)} copy-done((f32[2048,64]{0,1:T(8,128)S(1)}, f32[2048,64]{0,1:T(8,128)}, u32[]{:S(2)}) %copy-start) | copy-done | bytes 524312
  1.0 0.0 copy-start.1
  1.0 0.8 copy-done.1
  1.9 82.9 %shard_map.37 = f32[2048,512]{1,0:T(8,128)S(1)} custom-call(f32[2048,512]{1,0:T(8,128)} %z_hbm.1, f32[64,2048]{1,0:T(8,128)S(1)} %bitcast.1, f32[64,256]{1,0:T(8,128)S(1)} %copy-done.1), custom_call_target="tpu_custom_call" | custom-call | tf_op jit(solution)/shard_map/pallas_call | solution.py:338
  84.8 2.0 %copy.5 = f32[2048,512]{1,0:T(8,128)} copy(f32[2048,512]{1,0:T(8,128)S(1)} %shard_map.37) | data formatting | bytes 8388608
Async XLA Ops:
  0.0 1.0 %copy-start = (f32[2048,64]{0,1:T(8,128)S(1)}, f32[2048,64]{0,1:T(8,128)}, u32[]{:S(2)}) copy-start(f32[2048,64]{0,1:T(8,128)} %param.4) | copy-start | bytes 1572868
  1.0 0.8 copy-start.1

commit v2 on v0

v2 whole, which is shorter than its diff:
```python
import functools

import jax
import jax.numpy as jnp
from jax import lax
from jax.experimental import pallas as pl
from jax.experimental.pallas import tpu as pltpu
from jax.sharding import PartitionSpec as P

MESH = pl.DeviceIdType.MESH
F32, BF16 = jnp.float32, jnp.bfloat16
PLANES = 8
ROWS = 32
CHIPS = 16
SLAB = 64
HALF = SLAB // 2
NN = (((1,), (0,)), ((), ()))
NT = (((1,), (1,)), ((), ()))
TN = (((0,), (0,)), ((), ()))
PARTS = ((6, 4), (4, 4), (2, 2), (2, 2), (2, 2))
LAST = len(PARTS) - 1
HEIGHTS = tuple(4 * pieces + 2 * grams for pieces, grams in PARTS)


def split(value):
    high = value.astype(BF16)
    return high, (value - high.astype(F32)).astype(BF16)


def product(left, right, dims):
    dot = functools.partial(lax.dot_general, dimension_numbers=dims, preferred_element_type=F32)
    return dot(left[0], right[0]) + (dot(left[1], right[0]) + dot(left[0], right[1]))


def stacked(left, right, dims):
    rows = left[0].shape[0]
    by_high = lax.dot_general(jnp.concatenate(left, axis=0), right[0], dims, preferred_element_type=F32)
    by_low = lax.dot_general(left[0], right[1], dims, preferred_element_type=F32)
    return by_high[:rows] + (by_high[rows:] + by_low)


def kernel(
    z_hbm, v_hbm, t_hbm, z_full, v_hi, v_lo, c_hi, c_lo,
    panel, z_hi, z_lo, z_sum, gram, t_in, t_mine, t_planes, t_all, t_full,
    local, ring_out, ring_in, t_sem, t_spread_sem, part_out, part_in, *buffers,
):
    z, p = lax.axis_index("pcol"), lax.axis_index("prow")
    chip, core = p // 2, lax.rem(p, 2)
    right, left = lax.rem(z + 1, PLANES), lax.rem(z + PLANES - 1, PLANES)
    twin = p + 1 - 2 * core
    count = len(PARTS)
    gives, mixes, takes, alls = (buffers[i * count : i * count + count] for i in range(4))

    def plane(offset):
        return lax.rem(z + offset, PLANES)

    def fellow(step):
        o = 10 + step
        o = o - 15 * (o // 16)
        return (lax.rem(p // 8 + o // 4, 4) * 4 + lax.rem(chip + lax.rem(o, 4), 4)) * 2 + core

    barrier = pltpu.get_barrier_semaphore()
    for offset in (1, 7, 2, 6, 3, 5, 4):
        pl.semaphore_signal(barrier, inc=1, device_id={"pcol": plane(offset)}, device_id_type=MESH)
    pl.semaphore_signal(barrier, inc=1, device_id={"prow": twin}, device_id_type=MESH)

    def greet(step, carry):
        pl.semaphore_signal(barrier, inc=1, device_id={"prow": fellow(step)}, device_id_type=MESH)
        return carry

    lax.fori_loop(0, CHIPS - 1, greet, 0)
    t_copy = pltpu.make_async_copy(t_hbm, t_in, local.at[0])
    own_copy = pltpu.make_async_copy(v_hbm, panel.at[z], local.at[1])
    z_copy = pltpu.make_async_copy(z_hbm, z_full, local.at[2])
    t_copy.start()
    own_copy.start()
    z_copy.start()
    pl.semaphore_wait(barrier, CHIPS + PLANES - 1)

    def ring(way, step, half):
        rows = pl.ds(half * HALF, HALF)
        ref = panel.at[plane(PLANES - step) if way == 0 else plane(step), rows]
        return pltpu.make_async_remote_copy(
            v_hbm.at[rows] if step == 0 else ref, ref, ring_out.at[way, step, half], ring_in.at[way, step, half],
            device_id={"pcol": right if way == 0 else left}, device_id_type=MESH,
        )

    def arrive(step, half):
        for way in range(2):
            ring(way, step, half).wait_recv()
            if step < 2 or half == way:
                ring(way, step + 1, half).start()

    for half in range(2):
        for way in range(2):
            ring(way, 0, half).start()

    t_copy.wait()
    for tile in range(CHIPS):
        t_mine[tile] = t_in[(tile // 2) * 8 : (tile // 2) * 8 + 8, (tile % 2) * 128 : (tile % 2) * 128 + 128]
    for offset in range(1, PLANES):
        pltpu.make_async_remote_copy(
            t_mine.at[chip], t_planes.at[z], t_sem.at[0], t_sem.at[1],
            device_id={"pcol": plane(offset)}, device_id_type=MESH,
        ).start()
    t_planes[z] = t_mine[chip]

    def t_wait_planes():
        ref = t_planes.at[pl.ds(0, PLANES - 1)]
        return pltpu.make_async_remote_copy(
            ref, ref, t_sem.at[0], t_sem.at[1], device_id={"pcol": right}, device_id_type=MESH
        )

    def t_wait():
        ref = t_all.at[pl.ds(0, CHIPS - 1)]
        return pltpu.make_async_remote_copy(
            ref, ref, t_spread_sem.at[0], t_spread_sem.at[1], device_id={"pcol": right}, device_id_type=MESH
        )

    def t_spread():
        t_wait_planes().wait_recv()

        def send(step, carry):
            pltpu.make_async_remote_copy(
                t_planes, t_all.at[chip], t_spread_sem.at[0], t_spread_sem.at[1],
                device_id={"prow": fellow(step)}, device_id_type=MESH,
            ).start()
            return carry

        lax.fori_loop(0, CHIPS - 1, send, 0)
        t_all[chip] = t_planes[...]

    def t_collect():
        t_wait().wait_recv()
        for tile in range(CHIPS):
            for slab in range(PLANES):
                t_full[
                    slab * SLAB + (tile // 2) * 8 : slab * SLAB + (tile // 2) * 8 + 8,
                    (tile % 2) * 128 : (tile % 2) * 128 + 128,
                ] = t_all[tile, slab]

    def to_twin(part, stage, source, target):
        return pltpu.make_async_remote_copy(
            source, target, part_out.at[part, stage], part_in.at[part, stage],
            device_id={"prow": twin}, device_id_type=MESH,
        )

    def to_fellows(part, stage, source, target):
        def send(step, carry):
            other = fellow(step)
            pltpu.make_async_remote_copy(
                source(other // 2), target, part_out.at[part, stage], part_in.at[part, stage],
                device_id={"prow": other}, device_id_type=MESH,
            ).start()
            return carry

        lax.fori_loop(0, CHIPS - 1, send, 0)

    def from_fellows(part, stage):
        ref = takes[part].at[pl.ds(0, CHIPS - 1)]
        return pltpu.make_async_remote_copy(
            ref, ref, part_out.at[part, stage], part_in.at[part, stage],
            device_id={"prow": twin}, device_id_type=MESH,
        )

    def mix_copy(part):
        if part < LAST:
            return to_twin(part, 0, gives[part].at[1 - core], mixes[part].at[0])
        return to_twin(part, 0, mixes[part].at[0], mixes[part].at[1])

    def back_copy(part):
        return to_twin(part, 3, alls[part].at[core], alls[part].at[core])

    def scatter(part):
        give, take = gives[part], takes[part]
        if part < LAST:
            mix_copy(part).wait_recv()
            mixes[part][1] = give[core] + mixes[part][0]
            give = mixes[part].at[1]
        to_fellows(part, 1, lambda other: give.at[other], take.at[chip])
        take[chip] = give[chip]

    def gather(part):
        from_fellows(part, 1).wait_recv()
        total = jnp.sum(takes[part][...], axis=0)
        if part < LAST:
            kept = alls[part].at[core]
        else:
            kept, mix = alls[part], mixes[part]
            mix[0] = total
            copy = mix_copy(part)
            copy.start()
            copy.wait_recv()
            total = total + mix[1]
        kept[chip] = total
        to_fellows(part, 2, lambda other: kept.at[chip], kept.at[chip])

    def give_back(part):
        from_fellows(part, 2).wait_recv()
        back_copy(part).start()

    def place(part, tile):
        return (tile % 2, tile // 2) if part < LAST else (tile // 2, tile % 2)

    def halves(slab, first=0, rows=SLAB):
        at = pl.ds(first, rows)
        v_hi[slab, at], v_lo[slab, at] = split(panel[slab, at])

    def gram_of(slab, first=0, rows=SLAB):
        at, others = pl.ds(first, rows), pl.ds(4 - 4 * (slab // 4), 4)
        whole = (v_hi[others].reshape(4 * SLAB, -1), v_lo[others].reshape(4 * SLAB, -1))
        return stacked((v_hi[slab, at], v_lo[slab, at]), whole, NT)

    def sums_of(pieces):
        high, low = ([ref[slab, pl.ds(first, rows)] for slab, first, rows in pieces] for ref in (v_hi, v_lo))
        together = functools.partial(jnp.concatenate, axis=0)
        return stacked((together(high), together(low)), (z_hi[...], z_lo[...]), NN)

    def lay(part, sums, grams):
        pieces, with_gram = PARTS[part]
        for index in range(pieces * 16):
            tile, slot = place(part, index % ROWS), index // ROWS * 8
            row, lane = index // 4 * 8, index % 4 * 128
            gives[part].at[*tile][slot : slot + 8] = sums[row : row + 8, lane : lane + 128]
        for index in range(with_gram * 16):
            tile, slot = place(part, index % ROWS), pieces * 4 + index // ROWS * 4
            row, lane = index // 2 * 4, index % 2 * 128
            gives[part].at[*tile][slot : slot + 4] = grams[row : row + 4, lane : lane + 128]

    def collect(part, slabs):
        if part < LAST:
            back_copy(part).wait_recv()
        else:
            from_fellows(part, 2).wait_recv()
        pieces, with_gram = PARTS[part]
        for index in range(pieces * 16):
            tile, slot = place(part, index % ROWS), index // ROWS * 8
            slab, first = slabs[index // 16]
            row, lane = first + index % 16 // 4 * 8, index % 4 * 128
            z_sum[slab, row : row + 8, lane : lane + 128] = alls[part][*tile, slot : slot + 8]
        for index in range(with_gram * 16):
            tile, slot = place(part, index % ROWS), pieces * 4 + index // ROWS * 4
            slab, first = slabs[pieces - with_gram + index // 16]
            row, lane = first + index % 16 // 2 * 4, index % 2 * 128
            gram[slab, row : row + 4, lane : lane + 128] = alls[part][*tile, slot : slot + 4]

    def both(slab):
        return [(slab, 0), (slab, HALF)]

    def compute(part, fresh, older=()):
        grams = []
        for piece in fresh:
            halves(*piece)
            grams.append(gram_of(*piece))
        lay(part, sums_of([*older, *fresh]), jnp.concatenate(grams, axis=0))
        if part < LAST:
            mix_copy(part).start()

    behind = [plane(PLANES - 1 - step) for step in range(3)]
    ahead = [plane(1 + step) for step in range(3)]
    late = plane(4)
    v_hi[...] = jnp.zeros_like(v_hi)
    v_lo[...] = jnp.zeros_like(v_lo)
    gram[z] = jnp.zeros_like(gram[z])
    own_copy.wait()
    halves(z)
    z_copy.wait()
    z_hi[...], z_lo[...] = split(z_full[...])

    arrive(0, 0)
    arrive(0, 1)
    compute(0, [(behind[0], 0, SLAB), (ahead[0], 0, SLAB)], [(z, 0, SLAB)])
    scatter(0)
    arrive(1, 0)
    gather(0)
    t_spread()
    arrive(1, 1)
    compute(1, [(behind[1], 0, SLAB), (ahead[1], 0, SLAB)])
    scatter(1)
    arrive(2, 0)
    compute(2, [(behind[2], 0, HALF), (ahead[2], 0, HALF)])
    give_back(0)
    gather(1)
    scatter(2)
    t_collect()
    arrive(2, 1)
    compute(3, [(behind[2], HALF, HALF), (ahead[2], HALF, HALF)])
    scatter(3)
    gather(2)
    ring(0, 3, 0).wait_recv()
    ring(1, 3, 1).wait_recv()
    compute(4, [(late, 0, SLAB)])
    scatter(4)
    give_back(1)
    gather(3)
    collect(0, both(z) + both(behind[0]) + both(ahead[0]))
    t_hi, t_lo = split(t_full[...])
    give_back(2)
    collect(1, both(behind[1]) + both(ahead[1]))
    gather(4)
    give_back(3)
    collect(2, [(behind[2], 0), (ahead[2], 0)])
    collect(3, [(behind[2], HALF), (ahead[2], HALF)])
    collect(4, both(late))

    sums = z_sum[...].reshape(2 * 4 * SLAB, -1)
    grams = split(gram[...].reshape(2 * 4 * SLAB, -1))
    upper, lower = slice(0, 4 * SLAB), slice(4 * SLAB, 8 * SLAB)
    second = product((t_hi[lower], t_lo[lower]), split(sums[lower]), NN)
    parted = split(second)
    crossed = product((grams[0][upper], grams[1][upper]), parted, NN) + product(
        (grams[0][lower], grams[1][lower]), parted, TN
    )
    first = product((t_hi[upper], t_lo[upper]), split(sums[upper] - crossed), NN)
    c_hi[lower], c_lo[lower] = parted
    c_hi[upper], c_lo[upper] = split(first)

    for step in range(4):
        for way in range(2):
            for half in range(2):
                if step < 3 or half == way:
                    ring(way, step, half).wait_send()
    t_wait_planes().wait_send()
    t_wait().wait_send()
    for part in range(count):
        mix_copy(part).wait_send()
        from_fellows(part, 1).wait_send()
        from_fellows(part, 2).wait_send()
        if part < LAST:
            back_copy(part).wait_send()


def finish(z_full, v_hi, v_lo, c_hi, c_lo, out, stage, sem):
    block = stage.shape[1]
    c = (c_hi[...], c_lo[...])
    copies = []
    for index in range(stage.shape[0]):
        at = pl.ds(index * block, block)
        v = tuple(ref[:, :, at].reshape(PLANES * SLAB, block) for ref in (v_hi, v_lo))
        stage[index] = z_full[at] - product(v, c, TN)
        copies.append(pltpu.make_async_copy(stage.at[index], out.at[at], sem.at[index]))
        copies[-1].start()
    for copy in copies:
        copy.wait()


def shards(eigvecs, reflectors, factors):
    rows, columns = eigvecs.shape
    width = PLANES * SLAB // 2
    scratch = [
        pltpu.VMEM((PLANES, SLAB, rows), F32),
        pltpu.VMEM((rows, columns), BF16),
        pltpu.VMEM((rows, columns), BF16),
        pltpu.VMEM((PLANES, SLAB, columns), F32),
        pltpu.VMEM((PLANES, SLAB, width), F32),
        pltpu.VMEM((SLAB, width), F32),
        pltpu.VMEM((CHIPS, 8, 128), F32),
        pltpu.VMEM((PLANES, 8, 128), F32),
        pltpu.VMEM((CHIPS, PLANES, 8, 128), F32),
        pltpu.VMEM((PLANES * SLAB, width), F32),
        pltpu.SemaphoreType.DMA((3,)),
        pltpu.SemaphoreType.DMA((2, 4, 2)),
        pltpu.SemaphoreType.DMA((2, 4, 2)),
        pltpu.SemaphoreType.DMA((2,)),
        pltpu.SemaphoreType.DMA((2,)),
        pltpu.SemaphoreType.DMA((len(PARTS), 4)),
        pltpu.SemaphoreType.DMA((len(PARTS), 4)),
    ]
    early, last = HEIGHTS[:-1], HEIGHTS[-1]
    scratch += [pltpu.VMEM((2, CHIPS, height, 128), F32) for height in early]
    scratch += [pltpu.VMEM((CHIPS, 2, last, 128), F32)]
    scratch += [pltpu.VMEM((2, CHIPS, height, 128), F32) for height in early]
    scratch += [pltpu.VMEM((2, 2, last, 128), F32)]
    scratch += [pltpu.VMEM((CHIPS, height, 128), F32) for height in early]
    scratch += [pltpu.VMEM((CHIPS, 2, last, 128), F32)]
    scratch += [pltpu.VMEM((2, CHIPS, height, 128), F32) for height in early]
    scratch += [pltpu.VMEM((CHIPS, 2, last, 128), F32)]
    held = pl.pallas_call(
        kernel,
        out_shape=[
            jax.ShapeDtypeStruct((rows, columns), F32),
            jax.ShapeDtypeStruct((PLANES, SLAB, rows), BF16),
            jax.ShapeDtypeStruct((PLANES, SLAB, rows), BF16),
            jax.ShapeDtypeStruct((PLANES * SLAB, columns), BF16),
            jax.ShapeDtypeStruct((PLANES * SLAB, columns), BF16),
        ],
        in_specs=[pl.BlockSpec(memory_space=pltpu.HBM)] * 3,
        out_specs=[pl.BlockSpec(memory_space=pltpu.VMEM)] * 5,
        scratch_shapes=scratch,
        compiler_params=pltpu.CompilerParams(
            collective_id=0, has_side_effects=True, vmem_limit_bytes=40 * 1024 * 1024
        ),
    )(*(pltpu.with_memory_space_constraint(array, pltpu.HBM) for array in (eigvecs, reflectors.T, factors)))
    blocks = 8
    return pl.pallas_call(
        finish,
        out_shape=jax.ShapeDtypeStruct((rows, columns), F32),
        in_specs=[pl.BlockSpec(memory_space=pltpu.VMEM)] * 5,
        out_specs=pl.BlockSpec(memory_space=pltpu.HBM),
        scratch_shapes=[
            pltpu.VMEM((blocks, rows // blocks, columns), F32),
            pltpu.SemaphoreType.DMA((blocks,)),
        ],
        compiler_params=pltpu.CompilerParams(vmem_limit_bytes=32 * 1024 * 1024),
    )(*held)


def solution(mesh):
    return jax.shard_map(
        shards,
        mesh=mesh,
        in_specs=(P("prow", "pcol"), P("prow", "pcol"), P("pcol", None)),
        out_specs=P("prow", "pcol"),
        check_vma=False,
    )
```

time: 337 us -> 76.8 us (0.23)
  waiting for transfers between devices: 262 us -> 0 us
  Pallas kernels: 0 us -> 76.5 us
  matrix products: 29 us -> 0 us
  blocking collectives: 19.8 us -> 0 us
  between operations: 13.2 us -> 0.17 us
  local copies, waits for them, and re-layouts: 12.7 us -> 0 us
    psum x2 -> x0, waiting for transfers between devices: 200 us -> none  [shards(): summed = lax.psum(partial_value, 'prow')]
    pallas_call x0 -> x2, Pallas kernels: none -> 76.5 us  [the longest x1 72.2 us: shards(): pl.pallas_call(kernel, out_shape=[jax.ShapeDtypeStruct((rows, columns), F...]
    all_gather x1 -> x0, waiting for transfers between devices: 60.5 us -> none  [shards(): lax.all_gather(reflectors, 'pcol', axis=1, tiled=True)]
    dot_general x6 -> x0, matrix products: 29 us -> none  [the longest x4 17.4 us: product(): jnp.dot(left, right, precision=lax.Precision.HIGHEST, preferred_element_t...]
    all_gather x1 -> x0, blocking collectives: 19.8 us -> none  [shards(): lax.all_gather(factors, 'pcol', axis=0, tiled=True)]
    unnamed x7 -> x0, local copies, waits for them, and re-layouts: 7.37 us -> none
    sub x1 -> x0, local copies, waits for them, and re-layouts: 5.34 us -> none  [shards(): vectors = vectors - product(block_panel, coeffs)]
  transfers between devices with their start and end apart: 3 -> 0, of which waited for: 3 -> 0; matrix products, arithmetic and copies ran while one was open for 2% -> 0% of each run, Pallas kernels for 0% -> 0%
where the time goes in v2:
time: 76.8 us; the launch traced here: 76.7 us
  Pallas kernels  76.5 us (100%)
    pallas_call x1, Pallas kernels, shards(): pl.pallas_call(kernel, out_shape=[jax.ShapeDtypeStruct((rows, columns), F...  72.2 us
    pallas_call x1, Pallas kernels, shards(): pl.pallas_call(finish, out_shape=jax.ShapeDtypeStruct((rows, columns), F3...  4.33 us

profile of v2, /device:TPU:1, one launch (start us, length us, event | category | flops | bytes accessed | tf_op | source)
XLA Modules:
  0.0 76.7 jit_solution(2296918103649699262)
XLA Ops:
  0.0 72.2 %shard_map.37 = (f32[2048,512]{1,0:T(8,128)S(1)}, bf16[8,64,2048]{2,1,0:T(8,128)(2,1)S(1)}, bf16[8,64,2048]{2,1,0:T(8,128)(2,1)S(1)}, bf16[512,512]{1,0:T(8,128)(2,1)S(1)}, bf16[512,512]{1,0:T(8,128)(2,1)S(1)}) custom-call(f32[2048,512]{1,0:T(8,128)} %z_hbm.1, f32[64,2048]{1,0:T(8,128)} %bitcast.1, f32[64,256]{1,0:T(8,128)} %t_hbm.1), custom_call_target="tpu_custom_call" | custom-call | tf_op jit(solution)/shard_map/pallas_call | solution.py:378
  72.2 4.3 %shard_map.38 = f32[2048,512]{1,0:T(8,128)} custom-call(f32[2048,512]{1,0:T(8,128)S(1)} %get-tuple-element.10.z_full, bf16[8,64,2048]{2,1,0:T(8,128)(2,1)S(1)} %get-tuple-element.11.v_hi, bf16[8,64,2048]{2,1,0:T(8,128)(2,1)S(1)} %get-tuple-element.12.v_lo, bf16[512,512]{1,0:T(8,128)(2,1)S(1)} %get-tuple-element.13.c_hi, ...), custom_call_target="tpu_custom_call" | custom-call | tf_op jit(solution)/shard_map/pallas_call | solution.py:395

commit v3 on v2

--- a/solution.py
+++ b/solution.py
@@ -42,40 +42,38 @@
 def kernel(
     z_hbm, v_hbm, t_hbm, z_full, v_hi, v_lo, c_hi, c_lo,
     panel, z_hi, z_lo, z_sum, gram, t_in, t_mine, t_planes, t_all, t_full,
-    local, ring_out, ring_in, t_sem, t_spread_sem, part_out, part_in, *buffers,
+    local, ring_out, ring_in, t_out, t_got, t_spread_sem, part_out, part_in, *buffers,
 ):
     z, p = lax.axis_index("pcol"), lax.axis_index("prow")
     chip, core = p // 2, lax.rem(p, 2)
     right, left = lax.rem(z + 1, PLANES), lax.rem(z + PLANES - 1, PLANES)
     twin = p + 1 - 2 * core
     count = len(PARTS)
-    gives, mixes, takes, alls = (buffers[i * count : i * count + count] for i in range(4))
+    gives, takes, alls = (buffers[i * count : i * count + count] for i in range(3))
+    mixes = buffers[3 * count :]
 
     def plane(offset):
         return lax.rem(z + offset, PLANES)
 
-    def fellow(step):
-        o = 10 + step
-        o = o - 15 * (o // 16)
-        return (lax.rem(p // 8 + o // 4, 4) * 4 + lax.rem(chip + lax.rem(o, 4), 4)) * 2 + core
+    ys, xs = ([lax.rem(at + offset, 4) for offset in range(4)] for at in (p // 8, chip))
+    offsets = [(y, x) for y in (2, 1, 3, 0) for x in (2, 1, 3, 0)]
+    offsets.sort(key=lambda at: -sum(min(step, 4 - step) for step in at))
+    fellows = [(ys[y] * 4 + xs[x]) * 2 + core for y, x in offsets[:-1]]
+    mates = [(ys[y] * 4 + xs[x]) * 2 + at for y, x in offsets for at in (1 - core, core)][:-1]
 
     barrier = pltpu.get_barrier_semaphore()
-    for offset in (1, 7, 2, 6, 3, 5, 4):
-        pl.semaphore_signal(barrier, inc=1, device_id={"pcol": plane(offset)}, device_id_type=MESH)
-    pl.semaphore_signal(barrier, inc=1, device_id={"prow": twin}, device_id_type=MESH)
-
-    def greet(step, carry):
-        pl.semaphore_signal(barrier, inc=1, device_id={"prow": fellow(step)}, device_id_type=MESH)
-        return carry
-
-    lax.fori_loop(0, CHIPS - 1, greet, 0)
+    for neighbour in (left, right):
+        pl.semaphore_signal(barrier, inc=1, device_id={"pcol": neighbour}, device_id_type=MESH)
+
+    for other in mates:
+        pl.semaphore_signal(barrier, inc=1, device_id={"prow": other}, device_id_type=MESH)
     t_copy = pltpu.make_async_copy(t_hbm, t_in, local.at[0])
     own_copy = pltpu.make_async_copy(v_hbm, panel.at[z], local.at[1])
     z_copy = pltpu.make_async_copy(z_hbm, z_full, local.at[2])
     t_copy.start()
     own_copy.start()
     z_copy.start()
-    pl.semaphore_wait(barrier, CHIPS + PLANES - 1)
+    pl.semaphore_wait(barrier, 2 + ROWS - 1)
 
     def ring(way, step, half):
         rows = pl.ds(half * HALF, HALF)
@@ -85,59 +83,58 @@
             device_id={"pcol": right if way == 0 else left}, device_id_type=MESH,
         )
 
-    def arrive(step, half):
-        for way in range(2):
+    def arrive(step, turn):
+        for way in range(2):
+            half = turn if way == 0 else 1 - turn
             ring(way, step, half).wait_recv()
-            if step < 2 or half == way:
+            if step < 2 or (step == 2 and half == way):
                 ring(way, step + 1, half).start()
 
-    for half in range(2):
-        for way in range(2):
-            ring(way, 0, half).start()
+    for turn in range(2):
+        for way in range(2):
+            ring(way, 0, turn if way == 0 else 1 - turn).start()
+
+    def t_ring(way, step):
+        ref = t_planes.at[plane(PLANES - step) if way == 0 else plane(step)]
+        return pltpu.make_async_remote_copy(
+            ref, ref, t_out.at[way, step], t_got.at[way, step],
+            device_id={"pcol": right if way == 0 else left}, device_id_type=MESH,
+        )
+
+    def t_arrive(step):
+        for way in range(2):
+            if step + way < 4:
+                t_ring(way, step).wait_recv()
+            if step + way < 3:
+                t_ring(way, step + 1).start()
 
     t_copy.wait()
-    for tile in range(CHIPS):
-        t_mine[tile] = t_in[(tile // 2) * 8 : (tile // 2) * 8 + 8, (tile % 2) * 128 : (tile % 2) * 128 + 128]
-    for offset in range(1, PLANES):
-        pltpu.make_async_remote_copy(
-            t_mine.at[chip], t_planes.at[z], t_sem.at[0], t_sem.at[1],
-            device_id={"pcol": plane(offset)}, device_id_type=MESH,
-        ).start()
-    t_planes[z] = t_mine[chip]
-
-    def t_wait_planes():
-        ref = t_planes.at[pl.ds(0, PLANES - 1)]
-        return pltpu.make_async_remote_copy(
-            ref, ref, t_sem.at[0], t_sem.at[1], device_id={"pcol": right}, device_id_type=MESH
-        )
-
+    for index in range(ROWS):
+        row, lane = index // 4 * 8 + index % 2 * 4, index // 2 % 2 * 128
+        t_mine[index] = t_in[row : row + 4, lane : lane + 128]
+    t_planes[z] = t_mine[p]
+    for way in range(2):
+        t_ring(way, 0).start()
     def t_wait():
-        ref = t_all.at[pl.ds(0, CHIPS - 1)]
+        ref = t_all.at[pl.ds(0, ROWS - 1)]
         return pltpu.make_async_remote_copy(
             ref, ref, t_spread_sem.at[0], t_spread_sem.at[1], device_id={"pcol": right}, device_id_type=MESH
         )
 
     def t_spread():
-        t_wait_planes().wait_recv()
-
-        def send(step, carry):
+        for other in mates:
             pltpu.make_async_remote_copy(
-                t_planes, t_all.at[chip], t_spread_sem.at[0], t_spread_sem.at[1],
-                device_id={"prow": fellow(step)}, device_id_type=MESH,
+                t_planes, t_all.at[p], t_spread_sem.at[0], t_spread_sem.at[1],
+                device_id={"prow": other}, device_id_type=MESH,
             ).start()
-            return carry
-
-        lax.fori_loop(0, CHIPS - 1, send, 0)
-        t_all[chip] = t_planes[...]
+        t_all[p] = t_planes[...]
 
     def t_collect():
         t_wait().wait_recv()
-        for tile in range(CHIPS):
+        for index in range(ROWS):
             for slab in range(PLANES):
-                t_full[
-                    slab * SLAB + (tile // 2) * 8 : slab * SLAB + (tile // 2) * 8 + 8,
-                    (tile % 2) * 128 : (tile % 2) * 128 + 128,
-                ] = t_all[tile, slab]
+                row, lane = slab * SLAB + index // 4 * 8 + index % 2 * 4, index // 2 % 2 * 128
+                t_full[row : row + 4, lane : lane + 128] = t_all[index, slab]
 
     def to_twin(part, stage, source, target):
         return pltpu.make_async_remote_copy(
@@ -145,62 +142,47 @@
             device_id={"prow": twin}, device_id_type=MESH,
         )
 
-    def to_fellows(part, stage, source, target):
-        def send(step, carry):
-            other = fellow(step)
+    def to_others(part, stage, source, target):
+        for other in fellows if part < LAST else mates:
             pltpu.make_async_remote_copy(
-                source(other // 2), target, part_out.at[part, stage], part_in.at[part, stage],
+                source(other // 2 if part < LAST else other), target, part_out.at[part, stage], part_in.at[part, stage],
                 device_id={"prow": other}, device_id_type=MESH,
             ).start()
-            return carry
-
-        lax.fori_loop(0, CHIPS - 1, send, 0)
-
-    def from_fellows(part, stage):
-        ref = takes[part].at[pl.ds(0, CHIPS - 1)]
+
+    def from_others(part, stage):
+        ref = takes[part].at[pl.ds(0, takes[part].shape[0] - 1)]
         return pltpu.make_async_remote_copy(
             ref, ref, part_out.at[part, stage], part_in.at[part, stage],
             device_id={"prow": twin}, device_id_type=MESH,
         )
 
     def mix_copy(part):
-        if part < LAST:
-            return to_twin(part, 0, gives[part].at[1 - core], mixes[part].at[0])
-        return to_twin(part, 0, mixes[part].at[0], mixes[part].at[1])
+        return to_twin(part, 0, gives[part].at[1 - core], mixes[part].at[0])
 
     def back_copy(part):
         return to_twin(part, 3, alls[part].at[core], alls[part].at[core])
 
     def scatter(part):
-        give, take = gives[part], takes[part]
+        give, take, me = gives[part], takes[part], chip if part < LAST else p
         if part < LAST:
             mix_copy(part).wait_recv()
             mixes[part][1] = give[core] + mixes[part][0]
             give = mixes[part].at[1]
-        to_fellows(part, 1, lambda other: give.at[other], take.at[chip])
-        take[chip] = give[chip]
+        to_others(part, 1, lambda other: give.at[other], take.at[me])
+        take[me] = give[me]
 
     def gather(part):
-        from_fellows(part, 1).wait_recv()
-        total = jnp.sum(takes[part][...], axis=0)
-        if part < LAST:
-            kept = alls[part].at[core]
-        else:
-            kept, mix = alls[part], mixes[part]
-            mix[0] = total
-            copy = mix_copy(part)
-            copy.start()
-            copy.wait_recv()
-            total = total + mix[1]
-        kept[chip] = total
-        to_fellows(part, 2, lambda other: kept.at[chip], kept.at[chip])
+        from_others(part, 1).wait_recv()
+        kept, me = (alls[part].at[core], chip) if part < LAST else (alls[part], p)
+        kept[me] = jnp.sum(takes[part][...], axis=0)
+        to_others(part, 2, lambda other: kept.at[me], kept.at[me])
 
     def give_back(part):
-        from_fellows(part, 2).wait_recv()
+        from_others(part, 2).wait_recv()
         back_copy(part).start()
 
     def place(part, tile):
-        return (tile % 2, tile // 2) if part < LAST else (tile // 2, tile % 2)
+        return (tile % 2, tile // 2) if part < LAST else (tile,)
 
     def halves(slab, first=0, rows=SLAB):
         at = pl.ds(first, rows)
@@ -231,7 +213,7 @@
         if part < LAST:
             back_copy(part).wait_recv()
         else:
-            from_fellows(part, 2).wait_recv()
+            from_others(part, 2).wait_recv()
         pieces, with_gram = PARTS[part]
         for index in range(pieces * 16):
             tile, slot = place(part, index % ROWS), index // ROWS * 8
@@ -268,39 +250,42 @@
     z_hi[...], z_lo[...] = split(z_full[...])
 
     arrive(0, 0)
+    t_arrive(0)
     arrive(0, 1)
     compute(0, [(behind[0], 0, SLAB), (ahead[0], 0, SLAB)], [(z, 0, SLAB)])
+    t_arrive(1)
+    arrive(1, 0)
     scatter(0)
-    arrive(1, 0)
-    gather(0)
-    t_spread()
+    t_arrive(2)
     arrive(1, 1)
     compute(1, [(behind[1], 0, SLAB), (ahead[1], 0, SLAB)])
+    gather(0)
+    t_arrive(3)
+    arrive(2, 0)
+    t_spread()
     scatter(1)
-    arrive(2, 0)
-    compute(2, [(behind[2], 0, HALF), (ahead[2], 0, HALF)])
+    compute(2, [(behind[2], 0, HALF), (ahead[2], HALF, HALF)])
+    scatter(2)
+    arrive(2, 1)
+    compute(3, [(behind[2], HALF, HALF), (ahead[2], 0, HALF)])
     give_back(0)
     gather(1)
-    scatter(2)
-    t_collect()
-    arrive(2, 1)
-    compute(3, [(behind[2], HALF, HALF), (ahead[2], HALF, HALF)])
     scatter(3)
     gather(2)
-    ring(0, 3, 0).wait_recv()
-    ring(1, 3, 1).wait_recv()
+    arrive(3, 0)
     compute(4, [(late, 0, SLAB)])
     scatter(4)
+    collect(0, both(z) + both(behind[0]) + both(ahead[0]))
+    gather(3)
+    t_collect()
+    t_hi, t_lo = split(t_full[...])
     give_back(1)
-    gather(3)
-    collect(0, both(z) + both(behind[0]) + both(ahead[0]))
-    t_hi, t_lo = split(t_full[...])
     give_back(2)
     collect(1, both(behind[1]) + both(ahead[1]))
     gather(4)
     give_back(3)
-    collect(2, [(behind[2], 0), (ahead[2], 0)])
-    collect(3, [(behind[2], HALF), (ahead[2], HALF)])
+    collect(2, [(behind[2], 0), (ahead[2], HALF)])
+    collect(3, [(behind[2], HALF), (ahead[2], 0)])
     collect(4, both(late))
 
     sums = z_sum[...].reshape(2 * 4 * SLAB, -1)
@@ -320,13 +305,16 @@
             for half in range(2):
                 if step < 3 or half == way:
                     ring(way, step, half).wait_send()
-    t_wait_planes().wait_send()
+    for step in range(4):
+        for way in range(2):
+            if step + way < 4:
+                t_ring(way, step).wait_send()
     t_wait().wait_send()
     for part in range(count):
-        mix_copy(part).wait_send()
-        from_fellows(part, 1).wait_send()
-        from_fellows(part, 2).wait_send()
+        from_others(part, 1).wait_send()
+        from_others(part, 2).wait_send()
         if part < LAST:
+            mix_copy(part).wait_send()
             back_copy(part).wait_send()
 
 
@@ -354,27 +342,23 @@
         pltpu.VMEM((PLANES, SLAB, columns), F32),
         pltpu.VMEM((PLANES, SLAB, width), F32),
         pltpu.VMEM((SLAB, width), F32),
-        pltpu.VMEM((CHIPS, 8, 128), F32),
-        pltpu.VMEM((PLANES, 8, 128), F32),
-        pltpu.VMEM((CHIPS, PLANES, 8, 128), F32),
+        pltpu.VMEM((ROWS, 4, 128), F32),
+        pltpu.VMEM((PLANES, 4, 128), F32),
+        pltpu.VMEM((ROWS, PLANES, 4, 128), F32),
         pltpu.VMEM((PLANES * SLAB, width), F32),
         pltpu.SemaphoreType.DMA((3,)),
         pltpu.SemaphoreType.DMA((2, 4, 2)),
         pltpu.SemaphoreType.DMA((2, 4, 2)),
-        pltpu.SemaphoreType.DMA((2,)),
+        pltpu.SemaphoreType.DMA((2, 4)),
+        pltpu.SemaphoreType.DMA((2, 4)),
         pltpu.SemaphoreType.DMA((2,)),
         pltpu.SemaphoreType.DMA((len(PARTS), 4)),
         pltpu.SemaphoreType.DMA((len(PARTS), 4)),
     ]
-    early, last = HEIGHTS[:-1], HEIGHTS[-1]
-    scratch += [pltpu.VMEM((2, CHIPS, height, 128), F32) for height in early]
-    scratch += [pltpu.VMEM((CHIPS, 2, last, 128), F32)]
-    scratch += [pltpu.VMEM((2, CHIPS, height, 128), F32) for height in early]
-    scratch += [pltpu.VMEM((2, 2, last, 128), F32)]
-    scratch += [pltpu.VMEM((CHIPS, height, 128), F32) for height in early]
-    scratch += [pltpu.VMEM((CHIPS, 2, last, 128), F32)]
-    scratch += [pltpu.VMEM((2, CHIPS, height, 128), F32) for height in early]
-    scratch += [pltpu.VMEM((CHIPS, 2, last, 128), F32)]
+    early, last = HEIGHTS[:-1], pltpu.VMEM((ROWS, HEIGHTS[-1], 128), F32)
+    paired = [pltpu.VMEM((2, CHIPS, height, 128), F32) for height in early]
+    single = [pltpu.VMEM((CHIPS, height, 128), F32) for height in early]
+    scratch += [*paired, last, *single, last, *paired, last, *paired]
     held = pl.pallas_call(
         kernel,
         out_shape=[

time: 76.8 us -> 73.2 us (0.953)
  Pallas kernels: 76.5 us -> 72.9 us
    pallas_call x1, Pallas kernels: 72.2 us -> 68.6 us  [shards(): pl.pallas_call(kernel, out_shape=[jax.ShapeDtypeStruct((rows, columns), F...]
where the time goes in v3:
time: 73.2 us; the launch traced here: 73.1 us
  Pallas kernels  72.9 us (100%)
    pallas_call x1, Pallas kernels, shards(): pl.pallas_call(kernel, out_shape=[jax.ShapeDtypeStruct((rows, columns), F...  68.6 us
    pallas_call x1, Pallas kernels, shards(): pl.pallas_call(finish, out_shape=jax.ShapeDtypeStruct((rows, columns), F3...  4.33 us

profile of v3, /device:TPU:1, one launch (start us, length us, event | category | flops | bytes accessed | tf_op | source)
XLA Modules:
  0.0 73.1 jit_solution(10414161848053818128)
XLA Ops:
  0.0 68.6 %shard_map.37 = (f32[2048,512]{1,0:T(8,128)S(1)}, bf16[8,64,2048]{2,1,0:T(8,128)(2,1)S(1)}, bf16[8,64,2048]{2,1,0:T(8,128)(2,1)S(1)}, bf16[512,512]{1,0:T(8,128)(2,1)S(1)}, bf16[512,512]{1,0:T(8,128)(2,1)S(1)}) custom-call(f32[2048,512]{1,0:T(8,128)} %z_hbm.1, f32[64,2048]{1,0:T(8,128)} %bitcast.1, f32[64,256]{1,0:T(8,128)} %t_hbm.1), custom_call_target="tpu_custom_call" | custom-call | tf_op jit(solution)/shard_map/pallas_call | solution.py:362
  68.6 4.3 %shard_map.38 = f32[2048,512]{1,0:T(8,128)} custom-call(f32[2048,512]{1,0:T(8,128)S(1)} %get-tuple-element.10.z_full, bf16[8,64,2048]{2,1,0:T(8,128)(2,1)S(1)} %get-tuple-element.11.v_hi, bf16[8,64,2048]{2,1,0:T(8,128)(2,1)S(1)} %get-tuple-element.12.v_lo, bf16[512,512]{1,0:T(8,128)(2,1)S(1)} %get-tuple-element.13.c_hi, ...), custom_call_target="tpu_custom_call" | custom-call | tf_op jit(solution)/shard_map/pallas_call | solution.py:379

commit v4 on v3

v4 whole, which is shorter than its diff:
```python
import functools

import jax
import jax.numpy as jnp
from jax import lax
from jax.experimental import pallas as pl
from jax.experimental.pallas import tpu as pltpu
from jax.sharding import PartitionSpec as P

MESH = pl.DeviceIdType.MESH
F32, BF16 = jnp.float32, jnp.bfloat16
PLANES = 8
ROWS = 32
CHIPS = 16
SLAB = 64
HALF = SLAB // 2
NN = (((1,), (0,)), ((), ()))
NT = (((1,), (1,)), ((), ()))
TN = (((0,), (0,)), ((), ()))
PARTS = (6, 4, 2, 2, 2)
LAST = len(PARTS) - 1
HEIGHTS = tuple(4 * pieces for pieces in PARTS)


def split(value):
    high = value.astype(BF16)
    return high, (value - high.astype(F32)).astype(BF16)


def product(left, right, dims):
    dot = functools.partial(lax.dot_general, dimension_numbers=dims, preferred_element_type=F32)
    return dot(left[0], right[0]) + (dot(left[1], right[0]) + dot(left[0], right[1]))


def stacked(left, right, dims):
    rows = left[0].shape[0]
    by_high = lax.dot_general(jnp.concatenate(left, axis=0), right[0], dims, preferred_element_type=F32)
    by_low = lax.dot_general(left[0], right[1], dims, preferred_element_type=F32)
    return by_high[:rows] + (by_high[rows:] + by_low)


def kernel(
    z_hbm, v_hbm, t_hbm, z_full, u_hi, u_lo, w_hi, w_lo,
    panel, v_hi, v_lo, z_hi, z_lo, z_sum, z_late, t_in, t_mine, t_planes, t_all, t_full,
    g_give, g_take, g_planes, g_all, g_pairs, gram, turned,
    local, ring_out, ring_in, crossing, spread, part_out, part_in, *buffers,
):
    z, p = lax.axis_index("pcol"), lax.axis_index("prow")
    chip, core = p // 2, lax.rem(p, 2)
    right, left = lax.rem(z + 1, PLANES), lax.rem(z + PLANES - 1, PLANES)
    twin = p + 1 - 2 * core
    count = len(PARTS)
    gives, takes, alls = (buffers[i * count : i * count + count] for i in range(3))
    mixes = buffers[3 * count :]

    def plane(offset):
        return lax.rem(z + offset, PLANES)

    ys, xs = ([lax.rem(at + offset, 4) for offset in range(4)] for at in (p // 8, chip))
    offsets = [(y, x) for y in (2, 1, 3, 0) for x in (2, 1, 3, 0)]
    offsets.sort(key=lambda at: -sum(min(step, 4 - step) for step in at))
    fellows = [(ys[y] * 4 + xs[x]) * 2 + core for y, x in offsets[:-1]]
    mates = [(ys[y] * 4 + xs[x]) * 2 + at for y, x in offsets for at in (1 - core, core)][:-1]

    barrier = pltpu.get_barrier_semaphore()
    for offset in (1, 7, 2, 6, 3, 5, 4):
        pl.semaphore_signal(barrier, inc=1, device_id={"pcol": plane(offset)}, device_id_type=MESH)

    for other in mates:
        pl.semaphore_signal(barrier, inc=1, device_id={"prow": other}, device_id_type=MESH)
    t_copy = pltpu.make_async_copy(t_hbm, t_in, local.at[0])
    own_copy = pltpu.make_async_copy(v_hbm, panel.at[z], local.at[1])
    z_copy = pltpu.make_async_copy(z_hbm, z_full, local.at[2])
    t_copy.start()
    own_copy.start()
    z_copy.start()
    pl.semaphore_wait(barrier, PLANES - 1 + ROWS - 1)

    def ring(way, step, half):
        rows = pl.ds(half * HALF, HALF)
        ref = panel.at[plane(PLANES - step) if way == 0 else plane(step), rows]
        return pltpu.make_async_remote_copy(
            v_hbm.at[rows] if step == 0 else ref, ref, ring_out.at[way, step, half], ring_in.at[way, step, half],
            device_id={"pcol": right if way == 0 else left}, device_id_type=MESH,
        )

    def take(step, turn):
        for way in range(2):
            ring(way, step, turn if way == 0 else 1 - turn).wait_recv()

    def give(step, turn):
        for way in range(2):
            half = turn if way == 0 else 1 - turn
            if step < 3 or half == way:
                ring(way, step, half).start()

    give(0, 0)

    t_copy.wait()
    for index in range(ROWS):
        row, lane = index // 4 * 8 + index % 2 * 4, index // 2 % 2 * 128
        t_mine[index] = t_in[row : row + 4, lane : lane + 128]
    t_planes[z] = t_mine[p]

    def from_planes(target, stage):
        ref = target.at[pl.ds(0, PLANES - 1)]
        return pltpu.make_async_remote_copy(
            ref, ref, crossing.at[0, stage], crossing.at[1, stage], device_id={"pcol": right}, device_id_type=MESH
        )

    def to_planes(target, stage):
        for offset in (4, 3, 5, 2, 6, 1, 7):
            pltpu.make_async_remote_copy(
                target.at[z], target.at[z], crossing.at[0, stage], crossing.at[1, stage],
                device_id={"pcol": plane(offset)}, device_id_type=MESH,
            ).start()

    to_planes(t_planes, 0)
    give(0, 1)

    def from_mates(target, stage):
        ref = target.at[pl.ds(0, ROWS - 1)]
        return pltpu.make_async_remote_copy(
            ref, ref, spread.at[0, stage], spread.at[1, stage], device_id={"pcol": right}, device_id_type=MESH
        )

    def to_mates(source, target, stage):
        for other in mates:
            pltpu.make_async_remote_copy(
                source(other), target.at[p], spread.at[0, stage], spread.at[1, stage],
                device_id={"prow": other}, device_id_type=MESH,
            ).start()
        target[p] = source(p)[...]

    def t_spread():
        from_planes(t_planes, 0).wait_recv()
        to_mates(lambda other: t_planes, t_all, 0)

    def t_collect():
        from_mates(t_all, 0).wait_recv()
        for index in range(ROWS):
            for slab in range(PLANES):
                row, lane = slab * SLAB + index // 4 * 8 + index % 2 * 4, index // 2 % 2 * 128
                t_full[row : row + 4, lane : lane + 128] = t_all[index, slab]

    def g_scatter():
        left_side, right_side = (
            tuple(jnp.concatenate([ref[slab] for slab in slabs], axis=0) for ref in (v_hi, v_lo))
            for slabs in ((z, behind[1]), (ahead[0], ahead[1]))
        )
        pairs = stacked(left_side, right_side, NT)
        for index in range(ROWS):
            g_give[index] = pairs[index * 4 : index * 4 + 4]
        to_mates(lambda other: g_give.at[other], g_take, 1)

    def g_gather():
        from_mates(g_take, 1).wait_recv()
        g_planes[z] = jnp.sum(g_take[...], axis=0)
        to_planes(g_planes, 1)

    def g_spread():
        from_planes(g_planes, 1).wait_recv()
        to_mates(lambda other: g_planes, g_all, 2)

    def g_collect():
        from_mates(g_all, 2).wait_recv()
        for index in range(ROWS):
            for w in range(PLANES):
                g_pairs[w, index * 4 : index * 4 + 4] = g_all[index, w]
        gram[...] = jnp.zeros_like(gram)
        for a in range(PLANES):
            for distance in range(1, 5):
                b = (a + distance) % PLANES
                if a // 4 == b // 4 or (distance == 4 and a > b):
                    continue
                w, row = (a, 0) if distance < 3 else ((a + 2) % PLANES, SLAB)
                lane = SLAB * (1 - distance % 2)
                gram[a * SLAB : a * SLAB + SLAB, b % 4 * SLAB : b % 4 * SLAB + SLAB] = g_pairs[
                    w, row : row + SLAB, lane : lane + SLAB
                ]

    def to_twin(part, stage, source, target):
        return pltpu.make_async_remote_copy(
            source, target, part_out.at[part, stage], part_in.at[part, stage],
            device_id={"prow": twin}, device_id_type=MESH,
        )

    def to_others(part, stage, source, target):
        for other in fellows if part < LAST else mates:
            pltpu.make_async_remote_copy(
                source(other // 2 if part < LAST else other), target, part_out.at[part, stage], part_in.at[part, stage],
                device_id={"prow": other}, device_id_type=MESH,
            ).start()

    def from_others(part, stage):
        ref = takes[part].at[pl.ds(0, takes[part].shape[0] - 1)]
        return pltpu.make_async_remote_copy(
            ref, ref, part_out.at[part, stage], part_in.at[part, stage],
            device_id={"prow": twin}, device_id_type=MESH,
        )

    def mix_copy(part):
        return to_twin(part, 0, gives[part].at[1 - core], mixes[part].at[0])

    def back_copy(part):
        return to_twin(part, 3, alls[part].at[core], alls[part].at[core])

    def scatter(part):
        source, target, me = gives[part], takes[part], chip if part < LAST else p
        if part < LAST:
            mix_copy(part).wait_recv()
            mixes[part][1] = source[core] + mixes[part][0]
            source = mixes[part].at[1]
        to_others(part, 1, lambda other: source.at[other], target.at[me])
        target[me] = source[me]

    def gather(part):
        from_others(part, 1).wait_recv()
        kept, me = (alls[part].at[core], chip) if part < LAST else (alls[part], p)
        kept[me] = jnp.sum(takes[part][...], axis=0)
        to_others(part, 2, lambda other: kept.at[me], kept.at[me])

    def give_back(part):
        from_others(part, 2).wait_recv()
        back_copy(part).start()

    def place(part, tile):
        return (tile % 2, tile // 2) if part < LAST else (tile,)

    def halves(slab, first=0, rows=SLAB):
        at = pl.ds(first, rows)
        v_hi[slab, at], v_lo[slab, at] = split(panel[slab, at])

    def sums_of(pieces):
        high, low = ([ref[slab, pl.ds(first, rows)] for slab, first, rows in pieces] for ref in (v_hi, v_lo))
        together = functools.partial(jnp.concatenate, axis=0)
        return stacked((together(high), together(low)), (z_hi[...], z_lo[...]), NN)

    def lay(part, sums):
        for index in range(PARTS[part] * 16):
            tile, slot = place(part, index % ROWS), index // ROWS * 8
            row, lane = index // 4 * 8, index % 4 * 128
            gives[part].at[*tile][slot : slot + 8] = sums[row : row + 8, lane : lane + 128]

    def landed(part):
        return back_copy(part) if part < LAST else from_others(part, 2)

    def collect(part, slabs):
        landed(part).wait_recv()
        for index in range(PARTS[part] * 16):
            tile, slot = place(part, index % ROWS), index // ROWS * 8
            slab, first = slabs[index // 16]
            row, lane = first + index % 16 // 4 * 8, index % 4 * 128
            z_sum[slab, row : row + 8, lane : lane + 128] = alls[part][*tile, slot : slot + 8]

    def collect_late(part, first):
        landed(part).wait_recv()
        for index in range(PARTS[part] * 16):
            tile, row, lane = place(part, index), first + index // 4 * 8, index % 4 * 128
            z_late[row : row + 8, lane : lane + 128] = alls[part][*tile]

    def both(slab):
        return [(slab, 0), (slab, HALF)]

    def compute(part, fresh, older=()):
        for piece in fresh:
            halves(*piece)
        lay(part, sums_of([*older, *fresh]))
        if part < LAST:
            mix_copy(part).start()

    behind = [plane(PLANES - 1 - step) for step in range(3)]
    ahead = [plane(1 + step) for step in range(3)]
    late = plane(4)
    z_sum[...] = jnp.zeros_like(z_sum)
    own_copy.wait()
    halves(z)
    z_copy.wait()
    z_hi[...], z_lo[...] = split(z_full[...])

    take(0, 0)
    give(1, 0)
    t_spread()
    take(0, 1)
    give(1, 1)
    compute(0, [(behind[0], 0, SLAB), (ahead[0], 0, SLAB)], [(z, 0, SLAB)])
    scatter(0)
    take(1, 0)
    give(2, 0)
    take(1, 1)
    give(2, 1)
    halves(behind[1])
    halves(ahead[1])
    g_scatter()
    compute(1, [], [(behind[1], 0, SLAB), (ahead[1], 0, SLAB)])
    gather(0)
    scatter(1)
    take(2, 0)
    g_gather()
    give(3, 0)
    compute(2, [(behind[2], 0, HALF), (ahead[2], HALF, HALF)])
    give_back(0)
    gather(1)
    scatter(2)
    take(2, 1)
    compute(3, [(behind[2], HALF, HALF), (ahead[2], 0, HALF)])
    g_spread()
    scatter(3)
    gather(2)
    give_back(1)
    collect(0, both(z) + both(behind[0]) + both(ahead[0]))
    t_collect()
    t_halves = split(t_full[...])
    take(3, 0)
    compute(4, [(late, 0, SLAB)])
    scatter(4)
    gather(3)
    collect(1, both(behind[1]) + both(ahead[1]))

    g_collect()
    upper, lower = slice(0, 4 * SLAB), slice(4 * SLAB, 8 * SLAB)
    first, second = (tuple(half[rows] for half in t_halves) for rows in (upper, lower))
    crossed = product(split(gram[upper] + gram[lower].T), second, NN)
    corner = -product(first, split(crossed), NN)
    none = jnp.zeros_like(corner)
    m = jnp.concatenate(
        [jnp.concatenate([t_full[upper], corner], axis=1), jnp.concatenate([none, t_full[lower]], axis=1)], axis=0
    )
    turned[...] = m.T.reshape(turned.shape)
    coeff = split(product(split(m), split(z_sum[...].reshape(PLANES * SLAB, -1)), NN))
    block = 256

    def take_off(first, last):
        for index in range(first, last):
            at = pl.ds(index * block, block)
            v = tuple(ref[:, :, at].reshape(PLANES * SLAB, block) for ref in (v_hi, v_lo))
            z_full[at] = z_full[at] - product(v, coeff, TN)

    take_off(0, 2)
    give_back(2)
    gather(4)
    pieces = [(behind[2], 0, HALF), (ahead[2], HALF, HALF), (behind[2], HALF, HALF), (ahead[2], 0, HALF), (late, 0, SLAB)]
    m_late = [turned[slab, pl.ds(start, rows)] for slab, start, rows in pieces]
    m_late = split(jnp.concatenate([*m_late, jnp.zeros_like(turned[0])], axis=0).T)
    take_off(2, 5)
    give_back(3)
    take_off(5, 8)
    for index in range(z_full.shape[0] // block):
        at = pl.ds(index * block, block)
        v = tuple(ref[:, :, at].reshape(PLANES * SLAB, block) for ref in (v_hi, v_lo))
        u_hi[at], u_lo[at] = split(product(v, m_late, TN))
    z_late[3 * SLAB :] = jnp.zeros_like(z_late[3 * SLAB :])
    collect_late(2, 0)
    collect_late(3, SLAB)
    collect_late(4, 2 * SLAB)
    w_hi[...], w_lo[...] = split(z_late[...])

    for step in range(4):
        for way in range(2):
            for half in range(2):
                if step < 3 or half == way:
                    ring(way, step, half).wait_send()
    from_mates(t_all, 0).wait_send()
    from_mates(g_take, 1).wait_send()
    from_mates(g_all, 2).wait_send()
    from_planes(t_planes, 0).wait_send()
    from_planes(g_planes, 1).wait_send()
    for part in range(count):
        from_others(part, 1).wait_send()
        from_others(part, 2).wait_send()
        if part < LAST:
            mix_copy(part).wait_send()
            back_copy(part).wait_send()


def finish(part, u_hi, u_lo, w_hi, w_lo, out, stage, sem):
    block = stage.shape[1]
    w = jnp.concatenate([w_hi[...], w_hi[...], w_lo[...]], axis=0)
    copies = []
    for index in range(stage.shape[0]):
        at = pl.ds(index * block, block)
        u = jnp.concatenate([u_hi[at], u_lo[at], u_hi[at]], axis=1)
        stage[index] = part[at] - lax.dot_general(u, w, NN, preferred_element_type=F32)
        copies.append(pltpu.make_async_copy(stage.at[index], out.at[at], sem.at[index]))
        copies[-1].start()
    for copy in copies:
        copy.wait()


def shards(eigvecs, reflectors, factors):
    rows, columns = eigvecs.shape
    width = PLANES * SLAB // 2
    scratch = [
        pltpu.VMEM((PLANES, SLAB, rows), F32),
        pltpu.VMEM((PLANES, SLAB, rows), BF16),
        pltpu.VMEM((PLANES, SLAB, rows), BF16),
        pltpu.VMEM((rows, columns), BF16),
        pltpu.VMEM((rows, columns), BF16),
        pltpu.VMEM((PLANES, SLAB, columns), F32),
        pltpu.VMEM((4 * SLAB, columns), F32),
        pltpu.VMEM((SLAB, width), F32),
        pltpu.VMEM((ROWS, 4, 128), F32),
        pltpu.VMEM((PLANES, 4, 128), F32),
        pltpu.VMEM((ROWS, PLANES, 4, 128), F32),
        pltpu.VMEM((PLANES * SLAB, width), F32),
        pltpu.VMEM((ROWS, 4, 128), F32),
        pltpu.VMEM((ROWS, 4, 128), F32),
        pltpu.VMEM((PLANES, 4, 128), F32),
        pltpu.VMEM((ROWS, PLANES, 4, 128), F32),
        pltpu.VMEM((PLANES, 2 * SLAB, 2 * SLAB), F32),
        pltpu.VMEM((PLANES * SLAB, width), F32),
        pltpu.VMEM((PLANES, SLAB, PLANES * SLAB), F32),
        pltpu.SemaphoreType.DMA((3,)),
        pltpu.SemaphoreType.DMA((2, 4, 2)),
        pltpu.SemaphoreType.DMA((2, 4, 2)),
        pltpu.SemaphoreType.DMA((2, 2)),
        pltpu.SemaphoreType.DMA((2, 3)),
        pltpu.SemaphoreType.DMA((len(PARTS), 4)),
        pltpu.SemaphoreType.DMA((len(PARTS), 4)),
    ]
    early, last = HEIGHTS[:-1], pltpu.VMEM((ROWS, HEIGHTS[-1], 128), F32)
    paired = [pltpu.VMEM((2, CHIPS, height, 128), F32) for height in early]
    single = [pltpu.VMEM((CHIPS, height, 128), F32) for height in early]
    scratch += [*paired, last, *single, last, *paired, last, *paired]
    held = pl.pallas_call(
        kernel,
        out_shape=[
            jax.ShapeDtypeStruct((rows, columns), F32),
            jax.ShapeDtypeStruct((rows, 4 * SLAB), BF16),
            jax.ShapeDtypeStruct((rows, 4 * SLAB), BF16),
            jax.ShapeDtypeStruct((4 * SLAB, columns), BF16),
            jax.ShapeDtypeStruct((4 * SLAB, columns), BF16),
        ],
        in_specs=[pl.BlockSpec(memory_space=pltpu.HBM)] * 3,
        out_specs=[pl.BlockSpec(memory_space=pltpu.VMEM)] * 5,
        scratch_shapes=scratch,
        compiler_params=pltpu.CompilerParams(
            collective_id=0, has_side_effects=True, vmem_limit_bytes=40 * 1024 * 1024
        ),
    )(*(pltpu.with_memory_space_constraint(array, pltpu.HBM) for array in (eigvecs, reflectors.T, factors)))
    blocks = 8
    return pl.pallas_call(
        finish,
        out_shape=jax.ShapeDtypeStruct((rows, columns), F32),
        in_specs=[pl.BlockSpec(memory_space=pltpu.VMEM)] * 5,
        out_specs=pl.BlockSpec(memory_space=pltpu.HBM),
        scratch_shapes=[
            pltpu.VMEM((blocks, rows // blocks, columns), F32),
            pltpu.SemaphoreType.DMA((blocks,)),
        ],
        compiler_params=pltpu.CompilerParams(vmem_limit_bytes=32 * 1024 * 1024),
    )(*held)


def solution(mesh):
    return jax.shard_map(
        shards,
        mesh=mesh,
        in_specs=(P("prow", "pcol"), P("prow", "pcol"), P("pcol", None)),
        out_specs=P("prow", "pcol"),
        check_vma=False,
    )
```

time: 73.2 us -> 70.5 us (0.963)
  Pallas kernels: 72.9 us -> 70.3 us
    pallas_call x1, Pallas kernels: 4.33 us -> 2.66 us  [shards(): pl.pallas_call(finish, out_shape=jax.ShapeDtypeStruct((rows, columns), F3...]
    pallas_call x1, Pallas kernels: 68.6 us -> 67.6 us  [shards(): pl.pallas_call(kernel, out_shape=[jax.ShapeDtypeStruct((rows, columns), F...]
where the time goes in v4:
time: 70.5 us; the launch traced here: 70.4 us
  Pallas kernels  70.3 us (100%)
    pallas_call x1, Pallas kernels, shards(): pl.pallas_call(kernel, out_shape=[jax.ShapeDtypeStruct((rows, columns), F...  67.6 us
    pallas_call x1, Pallas kernels, shards(): pl.pallas_call(finish, out_shape=jax.ShapeDtypeStruct((rows, columns), F3...  2.66 us

profile of v4, /device:TPU:1, one launch (start us, length us, event | category | flops | bytes accessed | tf_op | source)
XLA Modules:
  0.0 70.4 jit_solution(12651201662518586917)
XLA Ops:
  0.0 67.6 %shard_map.37 = (f32[2048,512]{1,0:T(8,128)S(1)}, bf16[2048,256]{1,0:T(8,128)(2,1)S(1)}, bf16[2048,256]{1,0:T(8,128)(2,1)S(1)}, bf16[256,512]{1,0:T(8,128)(2,1)S(1)}, bf16[256,512]{1,0:T(8,128)(2,1)S(1)}) custom-call(f32[2048,512]{1,0:T(8,128)} %z_hbm.1, f32[64,2048]{1,0:T(8,128)} %bitcast.1, f32[64,256]{1,0:T(8,128)} %t_hbm.1), custom_call_target="tpu_custom_call" | custom-call | tf_op jit(solution)/shard_map/pallas_call | solution.py:425
  67.6 2.7 %shard_map.38 = f32[2048,512]{1,0:T(8,128)} custom-call(f32[2048,512]{1,0:T(8,128)S(1)} %get-tuple-element.10.part, bf16[2048,256]{1,0:T(8,128)(2,1)S(1)} %get-tuple-element.11.u_hi, bf16[2048,256]{1,0:T(8,128)(2,1)S(1)} %get-tuple-element.12.u_lo, bf16[256,512]{1,0:T(8,128)(2,1)S(1)} %get-tuple-element.13.w_hi, bf16[256,512]{1,0:T(8,128)(2,1)S(1)} %get-tuple-element.14.w_lo), custom_call_target="tpu_custom_call" | custom-call | tf_op jit(solution)/shard_map/pallas_call | solution.py:442

commit v5 on v4

--- a/solution.py
+++ b/solution.py
@@ -328,32 +328,28 @@
     )
     turned[...] = m.T.reshape(turned.shape)
     coeff = split(product(split(m), split(z_sum[...].reshape(PLANES * SLAB, -1)), NN))
-    block = 256
+    pieces = [(behind[2], 0, HALF), (ahead[2], HALF, HALF), (behind[2], HALF, HALF), (ahead[2], 0, HALF), (late, 0, SLAB)]
+    m_late = [turned[slab, pl.ds(start, rows)] for slab, start, rows in pieces]
+    m_late = split(jnp.concatenate([*m_late, jnp.zeros_like(turned[0])], axis=0).T)
+    sides = tuple(jnp.concatenate(both_sides, axis=1) for both_sides in zip(coeff, m_late))
+    block, columns = 256, z_full.shape[1]
 
     def take_off(first, last):
         for index in range(first, last):
             at = pl.ds(index * block, block)
             v = tuple(ref[:, :, at].reshape(PLANES * SLAB, block) for ref in (v_hi, v_lo))
-            z_full[at] = z_full[at] - product(v, coeff, TN)
-
-    take_off(0, 2)
+            share = product(v, sides, TN)
+            z_full[at] = z_full[at] - share[:, :columns]
+            u_hi[at], u_lo[at] = split(share[:, columns:])
+
     give_back(2)
     gather(4)
-    pieces = [(behind[2], 0, HALF), (ahead[2], HALF, HALF), (behind[2], HALF, HALF), (ahead[2], 0, HALF), (late, 0, SLAB)]
-    m_late = [turned[slab, pl.ds(start, rows)] for slab, start, rows in pieces]
-    m_late = split(jnp.concatenate([*m_late, jnp.zeros_like(turned[0])], axis=0).T)
-    take_off(2, 5)
+    take_off(0, 4)
     give_back(3)
-    take_off(5, 8)
-    for index in range(z_full.shape[0] // block):
-        at = pl.ds(index * block, block)
-        v = tuple(ref[:, :, at].reshape(PLANES * SLAB, block) for ref in (v_hi, v_lo))
-        u_hi[at], u_lo[at] = split(product(v, m_late, TN))
+    take_off(4, 8)
     z_late[3 * SLAB :] = jnp.zeros_like(z_late[3 * SLAB :])
     collect_late(2, 0)
     collect_late(3, SLAB)
-    collect_late(4, 2 * SLAB)
-    w_hi[...], w_lo[...] = split(z_late[...])
 
     for step in range(4):
         for way in range(2):
@@ -371,6 +367,8 @@
         if part < LAST:
             mix_copy(part).wait_send()
             back_copy(part).wait_send()
+    collect_late(4, 2 * SLAB)
+    w_hi[...], w_lo[...] = split(z_late[...])
 
 
 def finish(part, u_hi, u_lo, w_hi, w_lo, out, stage, sem):

time: 70.5 us -> 69.6 us (0.987)
  Pallas kernels: 70.3 us -> 69.4 us
    pallas_call x1, Pallas kernels: 67.6 us -> 66.7 us  [shards(): pl.pallas_call(kernel, out_shape=[jax.ShapeDtypeStruct((rows, columns), F...]
where the time goes in v5:
time: 69.6 us
  Pallas kernels  69.4 us (100%)
    pallas_call x1, Pallas kernels, shards(): pl.pallas_call(kernel, out_shape=[jax.ShapeDtypeStruct((rows, columns), F...  66.7 us
    pallas_call x1, Pallas kernels, shards(): pl.pallas_call(finish, out_shape=jax.ShapeDtypeStruct((rows, columns), F3...  2.66 us

profile of v5, /device:TPU:1, one launch (start us, length us, event | category | flops | bytes accessed | tf_op | source)
XLA Modules:
  0.0 69.6 jit_solution(4962979708061435529)
XLA Ops:
  0.0 66.7 %shard_map.37 = (f32[2048,512]{1,0:T(8,128)S(1)}, bf16[2048,256]{1,0:T(8,128)(2,1)S(1)}, bf16[2048,256]{1,0:T(8,128)(2,1)S(1)}, bf16[256,512]{1,0:T(8,128)(2,1)S(1)}, bf16[256,512]{1,0:T(8,128)(2,1)S(1)}) custom-call(f32[2048,512]{1,0:T(8,128)} %z_hbm.1, f32[64,2048]{1,0:T(8,128)} %bitcast.1, f32[64,256]{1,0:T(8,128)} %t_hbm.1), custom_call_target="tpu_custom_call" | custom-call | tf_op jit(solution)/shard_map/pallas_call | solution.py:423
  66.8 2.7 %shard_map.38 = f32[2048,512]{1,0:T(8,128)} custom-call(f32[2048,512]{1,0:T(8,128)S(1)} %get-tuple-element.10.part, bf16[2048,256]{1,0:T(8,128)(2,1)S(1)} %get-tuple-element.11.u_hi, bf16[2048,256]{1,0:T(8,128)(2,1)S(1)} %get-tuple-element.12.u_lo, bf16[256,512]{1,0:T(8,128)(2,1)S(1)} %get-tuple-element.13.w_hi, bf16[256,512]{1,0:T(8,128)(2,1)S(1)} %get-tuple-element.14.w_lo), custom_call_target="tpu_custom_call" | custom-call | tf_op jit(solution)/shard_map/pallas_call | solution.py:440

commit v6 on v5

--- a/solution.py
+++ b/solution.py
@@ -350,6 +350,7 @@
     z_late[3 * SLAB :] = jnp.zeros_like(z_late[3 * SLAB :])
     collect_late(2, 0)
     collect_late(3, SLAB)
+    w_hi[: 2 * SLAB], w_lo[: 2 * SLAB] = split(z_late[: 2 * SLAB])
 
     for step in range(4):
         for way in range(2):
@@ -368,7 +369,7 @@
             mix_copy(part).wait_send()
             back_copy(part).wait_send()
     collect_late(4, 2 * SLAB)
-    w_hi[...], w_lo[...] = split(z_late[...])
+    w_hi[2 * SLAB :], w_lo[2 * SLAB :] = split(z_late[2 * SLAB :])
 
 
 def finish(part, u_hi, u_lo, w_hi, w_lo, out, stage, sem):

time: 69.6 us -> 69.6 us (level)
  no operation moved by 1% of the time
where the time goes in v6:
time: 69.6 us; the launch traced here: 69.5 us
  Pallas kernels  69.4 us (100%)
    pallas_call x1, Pallas kernels, shards(): pl.pallas_call(kernel, out_shape=[jax.ShapeDtypeStruct((rows, columns), F...  66.7 us
    pallas_call x1, Pallas kernels, shards(): pl.pallas_call(finish, out_shape=jax.ShapeDtypeStruct((rows, columns), F3...  2.66 us

profile of v6, /device:TPU:1, one launch (start us, length us, event | category | flops | bytes accessed | tf_op | source)
XLA Modules:
  0.0 69.5 jit_solution(934046815343186265)
XLA Ops:
  0.0 66.7 %shard_map.37 = (f32[2048,512]{1,0:T(8,128)S(1)}, bf16[2048,256]{1,0:T(8,128)(2,1)S(1)}, bf16[2048,256]{1,0:T(8,128)(2,1)S(1)}, bf16[256,512]{1,0:T(8,128)(2,1)S(1)}, bf16[256,512]{1,0:T(8,128)(2,1)S(1)}) custom-call(f32[2048,512]{1,0:T(8,128)} %z_hbm.1, f32[64,2048]{1,0:T(8,128)} %bitcast.1, f32[64,256]{1,0:T(8,128)} %t_hbm.1), custom_call_target="tpu_custom_call" | custom-call | tf_op jit(solution)/shard_map/pallas_call | solution.py:424
  66.7 2.7 %shard_map.38 = f32[2048,512]{1,0:T(8,128)} custom-call(f32[2048,512]{1,0:T(8,128)S(1)} %get-tuple-element.10.part, bf16[2048,256]{1,0:T(8,128)(2,1)S(1)} %get-tuple-element.11.u_hi, bf16[2048,256]{1,0:T(8,128)(2,1)S(1)} %get-tuple-element.12.u_lo, bf16[256,512]{1,0:T(8,128)(2,1)S(1)} %get-tuple-element.13.w_hi, bf16[256,512]{1,0:T(8,128)(2,1)S(1)} %get-tuple-element.14.w_lo), custom_call_target="tpu_custom_call" | custom-call | tf_op jit(solution)/shard_map/pallas_call | solution.py:441
